TPU v7x, 32 devices: a whole 2x2x4 slice. The times are simulated.
32 devices in a mesh: groups: 2 (over x), chan: 16 (over z, y, core).
Axes of the slice: x: 2, y: 2, z: 4, core: 2. Of those that a mesh axis runs over, the one named last changes fastest.
Arguments:
- raw: bfloat16 [5120, 4096], P('chan', 'groups'), parts along dimension 1, may hold values from -50 to 50
- taps: bfloat16 [255], replicated, may hold values from -0.375 to 0.375
- tile_dist: int32 [16, 8], P('chan', 'groups'), parts along dimension 1, may hold values from 1 to 4, as said below
- tile_count: int32 [32], P(('groups', 'chan')), parts along dimension 0, may hold values from 0 to 4
- owner: int32 [8], P('groups'), parts along dimension 0, may hold values from 0 to 15, as said below
Outputs:
- band_stack: float32 [16, 256, 128], P('chan', 'groups'), parts along dimension 1
There are 2 independent parts, one for each index of `groups`. A program takes and returns all parts, laid end to end along the dimension named above; an argument that names none is the same for every part. Nothing has to cross between parts.
Inputs may be any that keep to these rules, and one draw needn't show every extreme that they name: Each row of tile_dist holds every distance of 1 to 4 once; in row i the first tile_count[i] entries d satisfy i + d < 16. `owner`: the owners are distinct, and some band is owned by index 15.
All inputs are finite; a program needn't handle non-finite values.
Results may differ from a plain program's by a relative error of at most 0.014.
Values may be sent and summed in bfloat16 or wider, within the bound.
A program may use at most 128 MiB of HBM per device.

v0:
```python
import math
import jax
import jax.numpy as jnp
from jax import lax
from jax.sharding import PartitionSpec as P


def extended(x, sides, width):
    for axis, dim in sides:
        size, length = (lax.axis_size(axis), x.shape[dim])
        up = [(i, (i + 1) % size) for i in range(size - 1)]
        down = [(j, i) for i, j in up]
        last = lax.slice_in_dim(x, length - width, length, axis=dim)
        initial = lax.slice_in_dim(x, 0, width, axis=dim)
        before = lax.ppermute(last, axis, up)
        after = lax.ppermute(initial, axis, down)
        x = jnp.concatenate([before, x, after], axis=dim)
    return x


def passed_along(x, axis, by):
    size = lax.axis_size(axis)
    pairs = [(i, i + by) for i in range(size) if 0 <= i + by < size]
    return lax.ppermute(x, axis, pairs)


def band_matrix(taps, out_rows, in_cols):
    width = taps.shape[0]
    offset = (
        jnp.arange(in_cols, dtype=jnp.int32)[None, :]
        - 5 * jnp.arange(out_rows, dtype=jnp.int32)[:, None]
    )
    inside = (offset >= 0) & (offset < width)
    picked = jnp.take(taps, jnp.clip(offset, 0, width - 1))
    return jnp.where(inside, picked, jnp.zeros_like(picked))


def whiten(block):
    length, channels = block.shape
    bins = length // 16
    freqs = jnp.arange(1, bins + 1, dtype=jnp.int32)[:, None]
    times = jnp.arange(length, dtype=jnp.int32)[None, :]
    angle = (freqs * times % length).astype(jnp.float32) * (2.0 * math.pi / length)
    table = jnp.concatenate([jnp.cos(angle), -jnp.sin(angle)], axis=0)
    table_high = table.astype(jnp.bfloat16)
    table_low = (table - table_high.astype(jnp.float32)).astype(jnp.bfloat16)
    spectrum = jnp.dot(table_high, block, preferred_element_type=jnp.float32)
    spectrum = spectrum + jnp.dot(table_low, block, preferred_element_type=jnp.float32)
    squares = spectrum * spectrum
    power = jnp.sum(squares[:bins] + squares[bins:], axis=1) / (2 * channels)
    gain = lax.rsqrt(power + 1e-06)
    return (spectrum * jnp.concatenate([gain, gain])[:, None]).astype(jnp.bfloat16)


def cross_tile(mine, partner, scale):
    product = lax.dot_general(
        mine, partner, (((0,), (0,)), ((), ())), preferred_element_type=jnp.float32
    )
    return product * scale


def shards(raw, taps, tile_dist, tile_count, owner):
    rows = raw.shape[0]
    width = taps.shape[0]
    half = (width - 1) // 2
    out_rows = rows // 5
    banded = band_matrix(taps, out_rows, rows + 2 * half)
    padded = extended(raw, (("chan", 0),), half)
    filtered = jnp.dot(banded, padded, preferred_element_type=jnp.float32)
    decimated = filtered.astype(jnp.bfloat16)
    regrouped = lax.all_to_all(decimated, "chan", split_axis=1, concat_axis=0, tiled=True)
    whitened = whiten(regrouped)
    channels = whitened.shape[1]
    scale = 1.0 / whitened.shape[0]
    bands = tile_dist.shape[1]
    slots = jnp.arange(bands, dtype=jnp.int32) < tile_count[0]
    partner = whitened
    stacks = []
    for distance in range(1, bands + 1):
        partner = passed_along(whitened, "chan", -distance)
        listed = jnp.sum(((tile_dist[0] == distance) & slots).astype(jnp.int32))
        tile = lax.cond(
            listed > 0,
            lambda first, second: cross_tile(first, second, scale),
            lambda first, second: jnp.zeros((channels, channels), jnp.float32),
            whitened,
            partner,
        )
        stacks.append(tile)
    stacked = jnp.stack(stacks)
    totals = lax.psum(stacked, "chan")
    selected = (owner == lax.axis_index("chan")).astype(jnp.float32)
    return jnp.einsum("b,bxy->xy", selected, totals, precision=lax.Precision.HIGHEST)[None]


def solution(mesh):
    in_specs = (P("chan", "groups"), P(), P("chan", "groups"), P(("groups", "chan")), P("groups"))
    out_specs = P("chan", "groups", None)
    return jax.shard_map(shards, mesh=mesh, in_specs=in_specs, out_specs=out_specs, check_vma=False)
```

profile of v0, /device:TPU:1, one launch (start us, length us, event | category | flops | bytes accessed | tf_op | source)
XLA Modules:
  0.0 350.2 jit_solution(16321516343890510298)
XLA Ops:
  6.5 1.3 fusion.63
  7.9 4.5 %collective-permute-start = (bf16[127,2048]{1,0:T(8,128)(2,1)S(1)}, bf16[127,2048]{1,0:T(8,128)(2,1)S(1)}, u32[]{:S(2)}, u32[]{:S(2)}) collective-permute-start(bf16[127,2048]{1,0:T(8,128)(2,1)S(1)} %get-tuple-element.49), channel_id=1, source_target_pairs={{0,1},{1,2},{2,3},{3,4},{4,5},{5,6},{6,7},{7,8},{8,9},{9,10},{10,1... | collective-permute-start | bytes 1560584 | tf_op jit(solution)/shard_map/ppermute | solution.py:15
  12.4 1.9 collective-permute-start.1
  14.4 0.1 compare_select_fusion
  14.5 0.2 reshape.83
  14.7 202.9 %gather_fusion = bf16[36736]{0:T(1024)(128)(2,1)S(1)} fusion(bf16[255]{0:T(256)(128)(2,1)S(1)} %copy-done, s32[36864]{0:T(1024)S(1)} %pad_clamp_fusion), kind=kCustom, calls=%fused_computation | custom fusion | bytes 293888 | tf_op jit(solution)/shard_map/jit(_take)/gather | solution.py:34
  217.7 0.2 reshape.82
  217.9 1.9 fusion.13
  219.8 0.8 copy.13
  220.6 6.5 %all-to-all-start = ((bf16[64,16,128]{2,0,1:T(8,128)(2,1)}), bf16[64,16,128]{2,0,1:T(8,128)(2,1)S(1)}, u32[]{:S(2)}, u32[]{:S(2)}) async-start(bf16[64,16,128]{2,0,1:T(8,128)(2,1)} %bitcast.58), calls=%async_computation | async-start | bytes 524288 | tf_op jit(solution)/shard_map/all_to_all | solution.py:71
  227.1 0.0 all-reduce.2.cloned.1.call-start
  227.8 1.1 fusion.35
  228.9 7.7 %all-to-all-done = bf16[64,16,128]{2,0,1:T(8,128)(2,1)S(1)} async-done(((bf16[64,16,128]{2,0,1:T(8,128)(2,1)}), bf16[64,16,128]{2,0,1:T(8,128)(2,1)S(1)}, u32[]{:S(2)}, u32[]{:S(2)}) %all-to-all-start) | async-done | bytes 262176 | tf_op jit(solution)/shard_map/all_to_all | solution.py:71
  236.5 0.2 fusion.17
  236.8 0.2 fusion.64
  237.0 0.1 fusion.43
  237.1 0.1 pad_maximum_fusion.2
  237.2 0.1 multiply_convert_fusion
  237.3 2.6 collective-permute-start.2
  239.9 1.3 collective-permute-start.3
  241.2 1.3 collective-permute-start.4
  242.5 1.3 collective-permute-start.5
  243.8 0.7 fusion.50
  247.1 0.2 conditional.5
  247.1 0.2 fusion.1
  247.3 0.5 collective-permute-done.4
  247.8 1.3 collective-permute-done.5
  249.2 0.2 conditional.7
  249.2 0.2 fusion.3
  249.4 0.7 pad_maximum_fusion.1
  250.1 91.1 %all-reduce.2.cloned.1.call-done = f32[4,128,128]{2,1,0:T(8,128)} async-done(((f32[4,128,128]{2,1,0:T(8,128)}), f32[4,128,128]{2,1,0:T(8,128)}) %all-reduce.2.cloned.1.call-update) | async-done | bytes 262160 | tf_op jit(solution)/shard_map/psum | solution.py:91
  341.3 2.1 fusion.22
  (21 shorter events, 0.1 us)
Async XLA Ops:
  6.5 8.2 %copy-start = (bf16[255]{0:T(256)(128)(2,1)S(1)}, bf16[255]{0:T(256)(128)(2,1)}, u32[]{:S(2)}) copy-start(bf16[255]{0:T(256)(128)(2,1)} %param.14) | copy-start | bytes 1534
  7.9 210.0 %collective-permute-start = (bf16[127,2048]{1,0:T(8,128)(2,1)S(1)}, bf16[127,2048]{1,0:T(8,128)(2,1)S(1)}, u32[]{:S(2)}, u32[]{:S(2)}) collective-permute-start(bf16[127,2048]{1,0:T(8,128)(2,1)S(1)} %get-tuple-element.49), channel_id=1, source_target_pairs={{0,1},{1,2},{2,3},{3,4},{4,5},{5,6},{6,7},{7,8},{8,9},{9,10},{10,1... | collective-permute-start | bytes 1560584 | tf_op jit(solution)/shard_map/ppermute | solution.py:15
  12.4 205.5 %collective-permute-start.1 = (bf16[127,2048]{1,0:T(8,128)(2,1)S(1)}, bf16[127,2048]{1,0:T(8,128)(2,1)}, u32[]{:S(2)}, u32[]{:S(2)}) collective-permute-start(bf16[127,2048]{1,0:T(8,128)(2,1)S(1)} %get-tuple-element.50), channel_id=1, source_target_pairs={{1,0},{2,1},{3,2},{4,3},{5,4},{6,5},{7,6},{8,7},{9,8},{10,9},{11,1... | collective-permute-start | bytes 1560584 | tf_op jit(solution)/shard_map/ppermute | solution.py:16
  14.7 203.2 %copy-start.1 = (bf16[320,2048]{1,0:T(8,128)(2,1)S(1)}, bf16[320,2048]{1,0:T(8,128)(2,1)}, u32[]{:S(2)}) copy-start(bf16[320,2048]{1,0:T(8,128)(2,1)} %param.13) | copy-start | bytes 3932164
  220.6 15.9 %all-to-all-start = ((bf16[64,16,128]{2,0,1:T(8,128)(2,1)}), bf16[64,16,128]{2,0,1:T(8,128)(2,1)S(1)}, u32[]{:S(2)}, u32[]{:S(2)}) async-start(bf16[64,16,128]{2,0,1:T(8,128)(2,1)} %bitcast.58), calls=%async_computation | async-start | bytes 524288 | tf_op jit(solution)/shard_map/all_to_all | solution.py:71
  227.0 16.7 %copy-start.3 = (s32[1,4]{1,0:T(1,128)S(1)}, s32[1,4]{1,0:T(1,128)}, u32[]{:S(2)}) copy-start(s32[1,4]{1,0:T(1,128)} %param.15) | copy-start | bytes 52
  227.1 114.2 %all-reduce.2.cloned.1.call-start = ((), (), s32[]{:S(2)}) async-start(), calls=%async_computation.1 | async-start | bytes 524288 | tf_op jit(solution)/shard_map/psum | solution.py:91
  236.8 104.5 %copy-start.2 = (s32[4]{0:T(128)S(1)}, s32[4]{0:T(128)}, u32[]{:S(2)}) copy-start(s32[4]{0:T(128)} %param.17) | copy-start | bytes 52
  237.3 9.7 %collective-permute-start.2 = (bf16[128,128]{1,0:T(8,128)(2,1)S(1)}, bf16[128,128]{1,0:T(8,128)(2,1)S(1)}, u32[]{:S(2)}, u32[]{:S(2)}) collective-permute-start(bf16[128,128]{1,0:T(8,128)(2,1)S(1)} %multiply_convert_fusion), channel_id=1, source_target_pairs={{1,0},{2,1},{3,2},{4,3},{5,4},{6,5},{7,6},{8,7},{9,8},{10,9},{11,1... | collective-permute-start | bytes 98312 | tf_op jit(solution)/shard_map/ppermute | solution.py:24
  239.9 7.2 %collective-permute-start.3 = (bf16[128,128]{1,0:T(8,128)(2,1)S(1)}, bf16[128,128]{1,0:T(8,128)(2,1)S(1)}, u32[]{:S(2)}, u32[]{:S(2)}) collective-permute-start(bf16[128,128]{1,0:T(8,128)(2,1)S(1)} %multiply_convert_fusion), channel_id=1, source_target_pairs={{2,0},{3,1},{4,2},{5,3},{6,4},{7,5},{8,6},{9,7},{10,8},{11,9},{12,... | collective-permute-start | bytes 98312 | tf_op jit(solution)/shard_map/ppermute | solution.py:24
  241.2 6.7 %collective-permute-start.4 = (bf16[128,128]{1,0:T(8,128)(2,1)S(1)}, bf16[128,128]{1,0:T(8,128)(2,1)S(1)}, u32[]{:S(2)}, u32[]{:S(2)}) collective-permute-start(bf16[128,128]{1,0:T(8,128)(2,1)S(1)} %multiply_convert_fusion), channel_id=1, source_target_pairs={{3,0},{4,1},{5,2},{6,3},{7,4},{8,5},{9,6},{10,7},{11,8},{12,9},{13... | collective-permute-start | bytes 98312 | tf_op jit(solution)/shard_map/ppermute | solution.py:24
  242.5 6.7 %collective-permute-start.5 = (bf16[128,128]{1,0:T(8,128)(2,1)S(1)}, bf16[128,128]{1,0:T(8,128)(2,1)S(1)}, u32[]{:S(2)}, u32[]{:S(2)}) collective-permute-start(bf16[128,128]{1,0:T(8,128)(2,1)S(1)} %multiply_convert_fusion), channel_id=1, source_target_pairs={{4,0},{5,1},{6,2},{7,3},{8,4},{9,5},{10,6},{11,7},{12,8},{13,9},{1... | collective-permute-start | bytes 98312 | tf_op jit(solution)/shard_map/ppermute | solution.py:24
Sparse Core Ops, SparseCore 0:
  250.2 90.9 all-reduce.1
where the time goes:
time: 351 us; the launch traced here: 350 us
  local copies, waits for them, and re-layouts  205 us (58%)
  waiting for transfers between devices  101 us (29%)
  starting transfers between devices  19.4 us (6%)
  between operations  16.8 us (5%)
  matrix products  4.78 us (1%)
    gather x2, local copies, waits for them, and re-layouts, band_matrix(): picked = jnp.take(taps, jnp.clip(offset, 0, width - 1))  203 us
    psum x1, waiting for transfers between devices, shards(): totals = lax.psum(stacked, 'chan')  91.1 us
    all_to_all x1, waiting for transfers between devices, shards(): lax.all_to_all(decimated, 'chan', split_axis=1, concat_axis=0, tiled=True)  7.67 us
  transfers between devices with their start and end apart: 8, of which 4 were waited for; matrix products, arithmetic and copies ran while one was open for 59% of the time, Pallas kernels for 0%

commit v1 on v0

--- a/solution.py
+++ b/solution.py
@@ -88,7 +88,7 @@
         )
         stacks.append(tile)
     stacked = jnp.stack(stacks)
-    totals = lax.psum(stacked, "chan")
+    totals = jnp.sum(lax.all_gather(stacked, "chan"), axis=0)
     selected = (owner == lax.axis_index("chan")).astype(jnp.float32)
     return jnp.einsum("b,bxy->xy", selected, totals, precision=lax.Precision.HIGHEST)[None]
 

time: 351 us -> 314 us (0.89)
  waiting for transfers between devices: 101 us -> 62.2 us
    psum x1 -> x0, waiting for transfers between devices: 91.1 us -> none  [shards(): totals = lax.psum(stacked, 'chan')]
    all_gather x0 -> x1, waiting for transfers between devices: none -> 52.6 us  [shards(): totals = jnp.sum(lax.all_gather(stacked, 'chan'), axis=0)]
  transfers between devices with their start and end apart: 8 -> 8, of which waited for: 4 -> 4; matrix products, arithmetic and copies ran while one was open for 59% -> 66% of each run, Pallas kernels for 0% -> 0%
where the time goes in v1:
time: 314 us; the launch traced here: 313 us
  local copies, waits for them, and re-layouts  205 us (65%)
  waiting for transfers between devices  62.2 us (20%)
  starting transfers between devices  19.4 us (6%)
  between operations  16.8 us (5%)
  other arithmetic  5.39 us (2%)
  matrix products  3.83 us (1%)
    gather x2, local copies, waits for them, and re-layouts, band_matrix(): picked = jnp.take(taps, jnp.clip(offset, 0, width - 1))  203 us
    all_gather x1, waiting for transfers between devices, shards(): totals = jnp.sum(lax.all_gather(stacked, 'chan'), axis=0)  52.6 us
    all_to_all x1, waiting for transfers between devices, shards(): lax.all_to_all(decimated, 'chan', split_axis=1, concat_axis=0, tiled=True)  7.68 us
    all_to_all x1, starting transfers between devices, shards(): lax.all_to_all(decimated, 'chan', split_axis=1, concat_axis=0, tiled=True)  6.45 us
    ppermute x4, starting transfers between devices, passed_along(): return lax.ppermute(x, axis, pairs)  6.44 us
  transfers between devices with their start and end apart: 8, of which 4 were waited for; matrix products, arithmetic and copies ran while one was open for 66% of the time, Pallas kernels for 0%

profile of v1, /device:TPU:1, one launch (start us, length us, event | category | flops | bytes accessed | tf_op | source)
XLA Modules:
  0.0 313.2 jit_solution(1108697610887840078)
XLA Ops:
  6.5 1.4 fusion.63
  7.9 4.5 %collective-permute-start = (bf16[127,2048]{1,0:T(8,128)(2,1)S(1)}, bf16[127,2048]{1,0:T(8,128)(2,1)S(1)}, u32[]{:S(2)}, u32[]{:S(2)}) collective-permute-start(bf16[127,2048]{1,0:T(8,128)(2,1)S(1)} %get-tuple-element.49), channel_id=1, source_target_pairs={{0,1},{1,2},{2,3},{3,4},{4,5},{5,6},{6,7},{7,8},{8,9},{9,10},{10,1... | collective-permute-start | bytes 1560584 | tf_op jit(solution)/shard_map/ppermute | solution.py:15
  12.5 1.9 collective-permute-start.1
  14.4 0.1 compare_select_fusion
  14.5 0.2 reshape.83
  14.8 202.9 %gather_fusion = bf16[36736]{0:T(1024)(128)(2,1)S(1)} fusion(bf16[255]{0:T(256)(128)(2,1)S(1)} %copy-done, s32[36864]{0:T(1024)S(1)} %pad_clamp_fusion), kind=kCustom, calls=%fused_computation | custom fusion | bytes 293888 | tf_op jit(solution)/shard_map/jit(_take)/gather | solution.py:34
  217.7 0.2 reshape.82
  218.0 1.9 fusion.13
  219.9 0.8 copy.14
  220.6 6.5 %all-to-all-start = ((bf16[64,16,128]{2,0,1:T(8,128)(2,1)}), bf16[64,16,128]{2,0,1:T(8,128)(2,1)S(1)}, u32[]{:S(2)}, u32[]{:S(2)}) async-start(bf16[64,16,128]{2,0,1:T(8,128)(2,1)} %bitcast.59), calls=%async_computation | async-start | bytes 524288 | tf_op jit(solution)/shard_map/all_to_all | solution.py:71
  227.8 1.1 fusion.35
  228.9 7.7 %all-to-all-done = bf16[64,16,128]{2,0,1:T(8,128)(2,1)S(1)} async-done(((bf16[64,16,128]{2,0,1:T(8,128)(2,1)}), bf16[64,16,128]{2,0,1:T(8,128)(2,1)S(1)}, u32[]{:S(2)}, u32[]{:S(2)}) %all-to-all-start) | async-done | bytes 262176 | tf_op jit(solution)/shard_map/all_to_all | solution.py:71
  236.6 0.2 fusion.17
  236.8 0.2 fusion.64
  237.0 0.1 fusion.43
  237.1 0.1 pad_maximum_fusion.2
  237.2 0.1 multiply_convert_fusion
  237.3 2.6 collective-permute-start.2
  239.9 1.3 collective-permute-start.3
  241.2 1.3 collective-permute-start.4
  242.5 1.3 collective-permute-start.5
  243.8 0.7 fusion.50
  247.1 0.2 conditional.5
  247.1 0.2 fusion.1
  247.3 0.6 collective-permute-done.4
  247.9 1.3 collective-permute-done.5
  249.2 0.2 conditional.7
  249.2 0.2 fusion.3
  249.4 0.7 pad_maximum_fusion.1
  250.2 52.6 %all-gather.3.cloned.1.call-done = f32[64,128,128]{2,1,0:T(8,128)} async-done(((f32[4,128,128]{2,1,0:T(8,128)}), f32[64,128,128]{2,1,0:T(8,128)}) %all-gather.3.cloned.1.call-update) | async-done | bytes 4194320 | tf_op jit(solution)/shard_map/all_gather | solution.py:91
  302.8 2.4 reduce_sum.59
  305.2 1.1 fusion.22
  (22 shorter events, 0.2 us)
Async XLA Ops:
  6.5 8.2 %copy-start = (bf16[255]{0:T(256)(128)(2,1)S(1)}, bf16[255]{0:T(256)(128)(2,1)}, u32[]{:S(2)}) copy-start(bf16[255]{0:T(256)(128)(2,1)} %param.14) | copy-start | bytes 1534
  7.9 210.0 %collective-permute-start = (bf16[127,2048]{1,0:T(8,128)(2,1)S(1)}, bf16[127,2048]{1,0:T(8,128)(2,1)S(1)}, u32[]{:S(2)}, u32[]{:S(2)}) collective-permute-start(bf16[127,2048]{1,0:T(8,128)(2,1)S(1)} %get-tuple-element.49), channel_id=1, source_target_pairs={{0,1},{1,2},{2,3},{3,4},{4,5},{5,6},{6,7},{7,8},{8,9},{9,10},{10,1... | collective-permute-start | bytes 1560584 | tf_op jit(solution)/shard_map/ppermute | solution.py:15
  12.5 205.5 %collective-permute-start.1 = (bf16[127,2048]{1,0:T(8,128)(2,1)S(1)}, bf16[127,2048]{1,0:T(8,128)(2,1)}, u32[]{:S(2)}, u32[]{:S(2)}) collective-permute-start(bf16[127,2048]{1,0:T(8,128)(2,1)S(1)} %get-tuple-element.50), channel_id=1, source_target_pairs={{1,0},{2,1},{3,2},{4,3},{5,4},{6,5},{7,6},{8,7},{9,8},{10,9},{11,1... | collective-permute-start | bytes 1560584 | tf_op jit(solution)/shard_map/ppermute | solution.py:16
  14.8 203.2 %copy-start.1 = (bf16[320,2048]{1,0:T(8,128)(2,1)S(1)}, bf16[320,2048]{1,0:T(8,128)(2,1)}, u32[]{:S(2)}) copy-start(bf16[320,2048]{1,0:T(8,128)(2,1)} %param.13) | copy-start | bytes 3932164
  219.8 23.9 %copy-start.3 = (s32[1,4]{1,0:T(1,128)S(1)}, s32[1,4]{1,0:T(1,128)}, u32[]{:S(2)}) copy-start(s32[1,4]{1,0:T(1,128)} %param.15) | copy-start | bytes 52
  220.6 15.9 %all-to-all-start = ((bf16[64,16,128]{2,0,1:T(8,128)(2,1)}), bf16[64,16,128]{2,0,1:T(8,128)(2,1)S(1)}, u32[]{:S(2)}, u32[]{:S(2)}) async-start(bf16[64,16,128]{2,0,1:T(8,128)(2,1)} %bitcast.59), calls=%async_computation | async-start | bytes 524288 | tf_op jit(solution)/shard_map/all_to_all | solution.py:71
  227.1 75.7 %all-gather.3.cloned.1.call-start = ((), (), s32[]{:S(2)}) async-start(), calls=%async_computation.1 | async-start | bytes 4456448 | tf_op jit(solution)/shard_map/all_gather | solution.py:91
  237.3 9.7 %collective-permute-start.2 = (bf16[128,128]{1,0:T(8,128)(2,1)S(1)}, bf16[128,128]{1,0:T(8,128)(2,1)S(1)}, u32[]{:S(2)}, u32[]{:S(2)}) collective-permute-start(bf16[128,128]{1,0:T(8,128)(2,1)S(1)} %multiply_convert_fusion), channel_id=1, source_target_pairs={{1,0},{2,1},{3,2},{4,3},{5,4},{6,5},{7,6},{8,7},{9,8},{10,9},{11,1... | collective-permute-start | bytes 98312 | tf_op jit(solution)/shard_map/ppermute | solution.py:24
  239.9 7.2 %collective-permute-start.3 = (bf16[128,128]{1,0:T(8,128)(2,1)S(1)}, bf16[128,128]{1,0:T(8,128)(2,1)S(1)}, u32[]{:S(2)}, u32[]{:S(2)}) collective-permute-start(bf16[128,128]{1,0:T(8,128)(2,1)S(1)} %multiply_convert_fusion), channel_id=1, source_target_pairs={{2,0},{3,1},{4,2},{5,3},{6,4},{7,5},{8,6},{9,7},{10,8},{11,9},{12,... | collective-permute-start | bytes 98312 | tf_op jit(solution)/shard_map/ppermute | solution.py:24
  241.2 6.7 %collective-permute-start.4 = (bf16[128,128]{1,0:T(8,128)(2,1)S(1)}, bf16[128,128]{1,0:T(8,128)(2,1)S(1)}, u32[]{:S(2)}, u32[]{:S(2)}) collective-permute-start(bf16[128,128]{1,0:T(8,128)(2,1)S(1)} %multiply_convert_fusion), channel_id=1, source_target_pairs={{3,0},{4,1},{5,2},{6,3},{7,4},{8,5},{9,6},{10,7},{11,8},{12,9},{13... | collective-permute-start | bytes 98312 | tf_op jit(solution)/shard_map/ppermute | solution.py:24
  242.5 6.7 %collective-permute-start.5 = (bf16[128,128]{1,0:T(8,128)(2,1)S(1)}, bf16[128,128]{1,0:T(8,128)(2,1)S(1)}, u32[]{:S(2)}, u32[]{:S(2)}) collective-permute-start(bf16[128,128]{1,0:T(8,128)(2,1)S(1)} %multiply_convert_fusion), channel_id=1, source_target_pairs={{4,0},{5,1},{6,2},{7,3},{8,4},{9,5},{10,6},{11,7},{12,8},{13,9},{1... | collective-permute-start | bytes 98312 | tf_op jit(solution)/shard_map/ppermute | solution.py:24
  250.1 55.1 %copy-start.2 = (s32[4]{0:T(128)S(1)}, s32[4]{0:T(128)}, u32[]{:S(2)}) copy-start(s32[4]{0:T(128)} %param.17) | copy-start | bytes 52
Sparse Core Ops, SparseCore 0:
  250.3 52.4 all-gather.2
